TPU v7x, 32 devices: a whole 2x2x4 slice. The times are simulated.
32 devices in a mesh: band: 8 (over y, x, core), col: 4 (over z).
Axes of the slice: x: 2, y: 2, z: 4, core: 2. Of those that a mesh axis runs over, the one named last changes fastest.
Arguments:
- valence: bfloat16 [8, 128, 128, 128], P('band', 'col'), may hold values from -6 to 6
- conduction: bfloat16 [24, 128, 128, 128], P('band', 'col'), may hold values from -6 to 6
- energy_val: float32 [8], replicated, may hold values from -12 to -2
- energy_cond: float32 [24], P('band'), may hold values from 1 to 20
- kept: int32 [3, 1536], replicated, may hold values from 0 to 127
- plan: int32 [3], replicated, may hold values from 0 to 7
Outputs:
- response: float32 [1536, 1536], P('band', 'col')
All inputs are finite; a program needn't handle non-finite values.
Results may differ from a plain program's by a relative error of at most 0.012.
Values may be sent and summed in bfloat16 or wider, within the bound.
No kernel may reach another device: no remote copies, remote signals or barrier semaphores. Data moves between devices by JAX's collectives and lax.ppermute only.
A program may use at most 192 MiB of HBM per device.

v0:
```python
import jax
import jax.numpy as jnp
from jax import lax
from jax.experimental import pallas as pl
from jax.experimental.pallas import tpu as pltpu
from jax.sharding import PartitionSpec as P

LANES = 128
NT = (((1,), (1,)), ((), ()))


def cas_of(phase, length):
    angle_value = 2.0 * jnp.pi / length * phase.astype(jnp.float32)
    return jnp.cos(angle_value) + jnp.sin(angle_value)


def spaced_rows(used):
    tiles = -(-used // 8)
    return 8 * (tiles + 1 - tiles % 2)


def round_kernel(index_ref, va_ref, vb_ref, c0_ref, c1_ref, table_ref, tx_ref, out_ref, s_ref, a_ref, g_ref):
    length = va_ref.shape[1]
    bands = c0_ref.shape[0]
    planes = c0_ref.shape[1]
    keep, lanes = tx_ref.shape
    used = 2 * bands * planes
    spaced = spaced_rows(used)
    table = table_ref[...]

    def transform_z(c_ref, v_ref, band_base, x_base):
        half = v_ref.shape[0]
        steps = half // 2

        def step(i, carry):
            band, x = i // steps, (i % steps) * 2
            product = (v_ref[pl.ds(x, 2)] * c_ref[band, pl.ds(x + x_base, 2)]).reshape(2 * length, length)
            out = lax.dot_general(table, product, NT, preferred_element_type=jnp.float32)
            out = out.astype(jnp.bfloat16).astype(jnp.float32)
            row = (band_base + band) * planes + x + x_base
            s_ref[pl.ds(row, length, stride=spaced), :] = out[:, :length]
            s_ref[pl.ds(row + 1, length, stride=spaced), :] = out[:, length:]
            return carry

        lax.fori_loop(0, bands * steps, step, 0, unroll=bands * steps)

    for c_ref, band_base in ((c0_ref, 0), (c1_ref, bands)):
        transform_z(c_ref, va_ref, band_base, 0)
        transform_z(c_ref, vb_ref, band_base, va_ref.shape[0])

    def transform_y(j, carry):
        base = pl.multiple_of(j * 2 * spaced, 8)
        rows = jnp.concatenate([s_ref[pl.ds(base, lanes), :], s_ref[pl.ds(base + spaced, lanes), :]])
        out = lax.dot_general(table, rows.astype(jnp.bfloat16), NT, preferred_element_type=jnp.float32)
        base = pl.multiple_of(j * 2 * length, 2 * length)
        a_ref[pl.ds(base, length), :] = out[:, :lanes]
        a_ref[pl.ds(base + length, length), :] = out[:, lanes:]
        return carry

    lax.fori_loop(0, length // 2, transform_y, 0, unroll=16)

    def pick(t, carry):
        rows = [a_ref[pl.ds(index_ref[t * 8 + k], 1), :] for k in range(8)]
        g_ref[pl.ds(pl.multiple_of(t * 8, 8), 8), :] = jnp.concatenate(rows)
        return carry

    lax.fori_loop(0, keep // 8, pick, 0, unroll=8)

    lane = lax.broadcasted_iota(jnp.int32, (keep, lanes), 1)
    scaled = jnp.where(lane < used, g_ref[...] * tx_ref[...], 0.0)
    high = scaled.astype(jnp.bfloat16)
    low = (scaled - high.astype(jnp.float32)).astype(jnp.bfloat16)
    rows = out_ref.shape[0]
    owner = lax.broadcasted_iota(jnp.int32, (rows, lanes), 1) // planes
    select = (owner == lax.broadcasted_iota(jnp.int32, (rows, lanes), 0)).astype(jnp.bfloat16)
    out_ref[...] = lax.dot_general(select, high, NT, preferred_element_type=jnp.float32) + lax.dot_general(
        select, low, NT, preferred_element_type=jnp.float32
    )


def round_coeffs(index, va, vb, c0, c1, table, tx):
    keep, lanes = tx.shape
    length = table.shape[0]
    rows = -(-2 * c0.shape[0] // 8) * 8
    vmem = pl.BlockSpec(memory_space=pltpu.VMEM)
    return pl.pallas_call(
        round_kernel,
        out_shape=jax.ShapeDtypeStruct((rows, keep), jnp.float32),
        in_specs=[pl.BlockSpec(memory_space=pltpu.SMEM)] + [vmem] * 6,
        out_specs=vmem,
        scratch_shapes=[
            pltpu.VMEM((length * spaced_rows(2 * c0.shape[0] * c0.shape[1]) + lanes, length), jnp.float32),
            pltpu.VMEM((length * length, lanes), jnp.float32),
            pltpu.VMEM((keep, lanes), jnp.float32),
        ],
        compiler_params=pltpu.CompilerParams(vmem_limit_bytes=18 * 2**20),
        cost_estimate=pl.CostEstimate(flops=4 * 10**9, bytes_accessed=12 * 2**20, transcendentals=0),
        name="round_coeffs",
    )(index, va, vb, c0, c1, table, tx)


def square_kernel(plan_ref, energy_val_ref, energy_cond_ref, flag_ref, weight_ref):
    rounds, bands = plan_ref.shape[0], energy_cond_ref.shape[0]
    me = lax.axis_index("band")
    side, group = me & 1, me >> 1
    plan = [plan_ref[r] for r in range(rounds)]

    def one(condition):
        return jnp.where(condition, 1, 0)

    def relative_of(band):
        return (band >> 1) ^ group

    at, own_side, repeated = jnp.int32(-1), jnp.int32(0), []
    for r in range(rounds):
        others = [plan[i] for i in range(rounds) if i != r]
        double = sum(one(band == (plan[r] ^ 1)) for band in others) > 0
        repeated.append(sum(one(band == plan[r]) for band in others) > 0)
        at = jnp.where(double, relative_of(plan[r]), at)
        own_side = jnp.where(relative_of(plan[r]) == 0, plan[r] & 1, own_side)

    def early_of(band):
        relative, low = relative_of(band), band & 1
        at_x = jnp.where(at == 1, 1 - low, 1)
        at_y = jnp.where(at == 2, low, 1)
        return jnp.where(relative == 0, 1, jnp.where(relative == 1, at_x, jnp.where(relative == 2, at_y, 0)))

    first, best = jnp.int32(0), jnp.int32(-1)
    for r in range(rounds):
        score = jnp.where(early_of(plan[r]) == 1, 2, one(repeated[r]))
        first = jnp.where(score > best, r, first)
        best = jnp.maximum(score, best)
    ordered = [plan[0]] + [jnp.where(first == r, plan[0], plan[r]) for r in range(1, rounds)]
    for r in range(1, rounds):
        ordered[0] = jnp.where(first == r, plan[r], ordered[0])

    own_double = one(at == 0)
    flags = [
        own_double,
        one(jnp.where(at == 0, 0, own_side) == side),
        one(jnp.where(at == 0, 1, own_side) == side),
        one(at >= 0),
        early_of(ordered[0]),
    ]
    for band in ordered:
        relative, low = relative_of(band), band & 1
        y_at_3 = jnp.where(at == 3, 1 - low, one(at == 1))
        x_at_3 = jnp.where(at == 3, low, one(at == 2))
        from_x = jnp.where(relative == 1, jnp.where(at == 1, low, 0), jnp.where(relative == 3, x_at_3, 0))
        from_y = jnp.where(relative == 2, jnp.where(at == 2, 1 - low, 0), jnp.where(relative == 3, y_at_3, 0))
        flags += [
            one(relative == 1),
            one(relative == 2),
            one((band & 1) == side),
            from_x,
            from_y,
            jnp.where(relative == 3, one(at <= 0), 0),
            one(band == ordered[0]),
        ]
    for k, flag in enumerate(flags):
        flag_ref[pl.ds(k, 1), :] = jnp.full((1, LANES), flag, jnp.int32)
    for r in range(rounds):
        for c in range(bands):
            gap = energy_cond_ref[c] - energy_val_ref[ordered[r]]
            weight_ref[pl.ds(r * bands + c, 1), :] = 1.0 / jnp.full((1, LANES), gap, jnp.float32)


def square_flags(plan, energy_val, energy_cond):
    rounds = plan.shape[0]
    smem = pl.BlockSpec(memory_space=pltpu.SMEM)
    vmem = pl.BlockSpec(memory_space=pltpu.VMEM)
    count = -(-(5 + 7 * rounds) // 8) * 8
    weight_rows = -(-rounds * energy_cond.shape[0] // 8) * 8
    return pl.pallas_call(
        square_kernel,
        out_shape=(
            jax.ShapeDtypeStruct((count, LANES), jnp.int32),
            jax.ShapeDtypeStruct((weight_rows, LANES), jnp.float32),
        ),
        in_specs=[smem] * 3,
        out_specs=(vmem, vmem),
        name="square_flags",
    )(plan, energy_val, energy_cond)


def per_device(valence, conduction, energy_val, energy_cond, kept, plan):
    band_local, x_local, length = conduction.shape[:3]
    keep = kept.shape[1]
    held = valence.shape[0]
    rounds = plan.shape[0]
    n_band = lax.axis_size("band")
    n_col = lax.axis_size("col")
    n_pair = n_band // 2
    bits = n_pair.bit_length() - 1
    me = lax.axis_index("band")
    side, group = me % 2, me // 2
    col = lax.axis_index("col")
    x_half = x_local // 2

    def swap(value, mask):
        return lax.ppermute(value, "band", [(i, i ^ mask) for i in range(n_band)])

    def half_of(value, which):
        return lax.dynamic_slice_in_dim(value, which * x_half, x_half, 1)

    cut = x_half // 2
    part_starts = (0, cut)

    def parts_of(which):
        return [lax.dynamic_slice_in_dim(valence, which * x_half + start, cut, 1) for start in part_starts]

    v_mine = parts_of(side)
    v_swapped = [swap(part, 1) for part in parts_of(1 - side)]
    square = held == 1 and bits == 2 and rounds > 1
    flags, square_weights = square_flags(plan, energy_val, energy_cond) if square else (plan, energy_val)
    v_swapped, conduction, flags = lax.optimization_barrier((v_swapped, conduction, flags))
    c_swapped = swap(half_of(conduction, 1 - side), 1)

    def prepared(conduction, kept):
        c_mine = half_of(conduction, side)
        position = jnp.arange(length, dtype=jnp.int32)
        table = cas_of(position[:, None] * position[None, :] % length, length).astype(jnp.bfloat16)
        used = 2 * band_local * x_half
        lanes = -(-used // LANES) * LANES
        x_global = col * x_local + side * x_half + jnp.arange(lanes, dtype=jnp.int32) % x_half
        tx = cas_of(kept[0][:, None] * x_global[None, :] % length, length) * length ** (-1.5)
        index = kept[2] * length + kept[1]
        c0 = jnp.where(side == 0, c_mine, c_swapped)
        c1 = jnp.where(side == 0, c_swapped, c_mine)
        return c0, c1, table, tx, index

    def coeffs_of(pair, c0, c1, table, tx, index):
        return round_coeffs(index, *pair, c0, c1, table, tx)

    def located(plan):
        plan_rows = jnp.broadcast_to(plan[:, None, None, None], (rounds, 1, 1, length))
        root = plan_rows // held
        return (root // 2) ^ group, root % 2 == side, plan_rows % held

    parts = list(zip(v_mine, v_swapped))

    def any_plan():
        relative, near_side, local = located(plan)
        ready = prepared(conduction, kept)
        is_target = plan[:, None] == jnp.arange(energy_val.shape[0], dtype=jnp.int32)[None, :]
        target_energy = jnp.sum(jnp.where(is_target, energy_val[None, :], 0.0), axis=1)
        weights = (1.0 / (energy_cond[None, :] - target_energy[:, None])).reshape(rounds * band_local, 1)

        def held_band(mine, swapped, r):
            band = jnp.where(near_side[r], mine[0], swapped[0])
            for i in range(1, held):
                band = jnp.where(local[r] == i, jnp.where(near_side[r], mine[i], swapped[i]), band)
            return band

        def nearer(r, bit, near, far):
            return jnp.where((relative[r] >> bit) & 1 == 0, near, far)

        orders = [list(range(bits)), list(range(bits))[::-1]]
        if 2 * held <= rounds and bits:
            far_mine = [swap(part[0], 2 << order[0]) for part, order in zip(parts, orders)]
            far_swapped = [swap(part[1], 2 << order[0]) for part, order in zip(parts, orders)]
            far_mine, far_swapped, ready = lax.optimization_barrier((far_mine, far_swapped, ready))
            slots = [
                [
                    nearer(r, order[0], held_band(*part, r), held_band(fm, fs, r))
                    for part, fm, fs, order in zip(parts, far_mine, far_swapped, orders)
                ]
                for r in range(rounds)
            ]
            slots = lax.optimization_barrier(slots)
            orders = [order[1:] for order in orders]
        else:
            slots = [[held_band(*part, r) for part in parts] for r in range(rounds)]
        for step in range(len(orders[0])):
            slots = [
                [nearer(r, order[step], value, swap(value, 2 << order[step])) for value, order in zip(slots[r], orders)]
                for r in range(rounds)
            ]
        return [coeffs_of(pair, *ready) for pair in slots], weights

    def four_pairs(flags, weights):
        def flag(k):
            return flags[k] != 0

        def round_flag(r, k):
            return flag(5 + 7 * r + k)

        def own(k):
            return [jnp.where(flag(k), part[0][0], part[1][0]) for part in parts]

        to_x, to_y = own(1), own(2)
        to_x, to_y, *given = lax.optimization_barrier((to_x, to_y, conduction, kept))
        x_a, y_b = swap(to_x[0], 2), swap(to_y[1], 4)
        x_b, y_a = swap(to_x[1], 2), swap(to_y[0], 4)
        ready = prepared(*given)
        x_a, y_b, ready = lax.optimization_barrier((x_a, y_b, ready))
        on_y, on_x = jnp.where(flag(0), to_x[0], x_a), jnp.where(flag(0), to_y[1], y_b)
        on_y, on_x, flags = lax.optimization_barrier((on_y, on_x, flags))
        on_y, on_x = swap(on_y, 4), swap(on_x, 2)

        def near(r, half, x, y):
            here = jnp.where(round_flag(r, 2), parts[half][0][0], parts[half][1][0])
            return jnp.where(round_flag(r, 0), x, jnp.where(round_flag(r, 1), y, here))

        partial = [coeffs_of((near(0, 0, x_a, y_a), near(0, 1, x_b, y_b)), *ready)]
        partial, on_x, on_y = lax.optimization_barrier((partial, on_x, on_y))
        later_x, later_y = jnp.where(flag(0), to_y[0], y_a), jnp.where(flag(0), to_x[1], x_b)
        last_x, last_y = lax.cond(
            flags[3, 0] != 0,
            lambda x, y: (swap(x, 2), swap(y, 4)),
            lambda x, y: (x, y),
            later_x,
            later_y,
        )
        for r in range(1, rounds):
            from_x, from_y, from_both = (round_flag(r, k) for k in (3, 4, 5))
            part_a = jnp.where(from_x, last_x, jnp.where(from_y | from_both, on_y, near(r, 0, x_a, y_a)))
            part_b = jnp.where(from_y, last_y, jnp.where(from_x | from_both, on_x, near(r, 1, x_b, y_b)))
            partial.append(coeffs_of((part_a, part_b), *ready))
        copied = partial[rounds - 1]
        for r in range(1, rounds - 1):
            copied = jnp.where(flags[5 + 7 * r + 6, :1] != 0, partial[r], copied)
        partial[0] = jnp.where(flags[4, :1] != 0, partial[0], copied)
        return partial, weights[: rounds * band_local, :1]

    partial, weights = four_pairs(flags, square_weights) if square else any_plan()

    first = jnp.concatenate([p[:band_local] for p in partial])
    second = jnp.concatenate([p[band_local : 2 * band_local] for p in partial])
    mine = jnp.where(side == 0, first, second)
    coeffs = mine + swap(jnp.where(side == 0, second, first), 1)
    sent = coeffs.astype(jnp.bfloat16)
    for shift in range(1, n_col):
        moved = lax.ppermute(sent, "col", [(i, (i + shift) % n_col) for i in range(n_col)])
        coeffs = coeffs + moved.astype(jnp.float32)
    weighted = (weights * coeffs).astype(jnp.bfloat16)
    plain = coeffs.astype(jnp.bfloat16)

    col_width, row_width = keep // n_col, keep // n_band
    col_piece = lax.dynamic_slice_in_dim(plain, col * col_width, col_width, 1)

    def rows_of(other):
        return lax.dynamic_slice_in_dim(weighted, other * 2 * row_width, 2 * row_width, 1)

    pieces = [jnp.concatenate([col_piece, rows_of(group)], axis=1)]
    for mask in range(1, n_pair):
        pieces.append(swap(jnp.concatenate([col_piece, rows_of(group ^ mask)], axis=1), 2 * mask))
    gathered = jnp.concatenate(pieces)
    columns = gathered[:, :col_width]
    rows_low, rows_high = gathered[:, col_width : col_width + row_width], gathered[:, col_width + row_width :]
    rows_mine = jnp.where(side == 0, rows_low, rows_high)
    rows_other = jnp.where(side == 0, rows_high, rows_low)
    swapped = swap(jnp.concatenate([columns, rows_other], axis=1), 1)
    columns = jnp.concatenate([columns, swapped[:, :col_width]])
    rows = jnp.concatenate([rows_mine, swapped[:, col_width:]])
    response_tile = lax.dot_general(
        rows, columns, (((0,), (0,)), ((), ())), preferred_element_type=jnp.float32
    )
    factor = (rounds * band_local * n_band) ** (-0.5)
    return -response_tile * factor


def solution(mesh):
    return jax.shard_map(
        per_device,
        mesh=mesh,
        in_specs=(
            P("band", "col", None, None),
            P("band", "col", None, None),
            P(),
            P("band"),
            P(),
            P(),
        ),
        out_specs=P("band", "col"),
        check_vma=False,
    )
```

profile of v0, /device:TPU:0, one launch (start us, length us, event | category | flops | bytes accessed | tf_op | source)
XLA Modules:
  0.0 66.2 jit_solution(2398301599752132346)
XLA Ops:
  0.0 1.1 %constant_dynamic-slice_fusion.5 = (bf16[1,8,128,128]{3,2,1,0:T(8,128)(2,1)S(1)}, bf16[1,8,128,128]{3,2,1,0:T(8,128)(2,1)S(1)}) fusion(bf16[1,32,128,128]{3,2,1,0:T(8,128)(2,1)} %param.8, s32[]{:T(128)S(6)} %select_n.212, s32[]{:T(128)S(6)} %select_n.211), kind=kLoop, calls=%fused_computation.86 | loop fusion | bytes 1048584 | tf_op jit(solution)/shard_map/dynamic_slice | solution.py:210
  1.1 0.5 collective-permute-start.2
  1.6 0.1 collective-permute-start.3
  1.7 1.4 %square_flags.1 = (s32[32,128]{1,0:T(8,128)}, f32[16,128]{1,0:T(8,128)}) custom-call(s32[3]{0:T(128)} %plan_ref.1, f32[8]{0:T(128)} %energy_val_ref.1, f32[3]{0:T(128)} %energy_cond_ref.1), custom_call_target="tpu_custom_call" | custom-call | tf_op jit(solution)/shard_map/square_flags/pallas_call | solution.py:174
  3.0 0.1 collective-permute-done.3
  3.1 1.6 %constant_dynamic-slice_fusion.4 = bf16[3,16,128,128]{3,2,1,0:T(8,128)(2,1)S(1)} fusion(bf16[3,32,128,128]{3,2,1,0:T(8,128)(2,1)} %param.9, s32[]{:T(128)S(6)} %select_n.211), kind=kLoop, calls=%fused_computation.85 | loop fusion | bytes 3145732 | tf_op jit(solution)/shard_map/dynamic_slice | solution.py:204
  4.7 0.5 collective-permute-start.6
  5.2 0.3 add_convert_fusion.table_ref
  5.5 0.1 bitcast_select_fusion.8
  5.6 2.7 %collective-permute-start.4 = (bf16[8,128,128]{2,1,0:T(8,128)(2,1)S(1)}, bf16[8,128,128]{2,1,0:T(8,128)(2,1)S(1)}, u32[]{:S(2)}, u32[]{:S(2)}) collective-permute-start(bf16[8,128,128]{2,1,0:T(8,128)(2,1)S(1)} %get-tuple-element.47), channel_id=1, source_target_pairs={{0,8},{4,12},{8,0},{12,4},{16,24},{20,28},{24,16},{28,20},{1,9},{5... | collective-permute-start | bytes 786440 | tf_op jit(solution)/shard_map/ppermute | solution.py:201
  8.3 1.5 %collective-permute-start.5 = (bf16[8,128,128]{2,1,0:T(8,128)(2,1)S(1)}, bf16[8,128,128]{2,1,0:T(8,128)(2,1)S(1)}, u32[]{:S(2)}, u32[]{:S(2)}) collective-permute-start(bf16[8,128,128]{2,1,0:T(8,128)(2,1)S(1)} %get-tuple-element.48), channel_id=1, source_target_pairs={{0,16},{4,20},{8,24},{12,28},{16,0},{20,4},{24,8},{28,12},{1,17},{... | collective-permute-start | bytes 786440 | tf_op jit(solution)/shard_map/ppermute | solution.py:201
  9.9 0.5 collective-permute-start.8
  10.5 3.2 %add_multiply_fusion.tx_ref = f32[1536,128]{1,0:T(8,128)S(1)} fusion(s32[128]{0:T(128)S(1)} %fusion.37, s32[1536]{0:T(1024)S(1)} %get-tuple-element.70), kind=kLoop, calls=%fused_computation.12 | loop fusion | flops 3145728 | bytes 793088 | tf_op jit(solution)/shard_map/mul | solution.py:226
  13.7 2.4 %broadcast_select_fusion = (bf16[3,16,128,128]{3,2,1,0:T(8,128)(2,1)S(1)}, bf16[3,16,128,128]{3,2,1,0:T(8,128)(2,1)S(1)}) fusion(bf16[3,16,128,128]{3,2,1,0:T(8,128)(2,1)} %collective-permute-done.6, pred[]{:T(512)S(6)} %eq.10, bf16[3,32,128,128]{3,2,1,0:T(8,128)(2,1)} %param.9, s32[]{:T(128)S(6)} %select_n.213), kind=kLoop, calls=%fused_computation | loop fusion | flops 1572864 | bytes 6291461 | tf_op jit(solution)/shard_map/jit(_where)/select_n | solution.py:229
  16.1 1.4 %collective-permute-done.5 = bf16[8,128,128]{2,1,0:T(8,128)(2,1)S(1)} collective-permute-done((bf16[8,128,128]{2,1,0:T(8,128)(2,1)S(1)}, bf16[8,128,128]{2,1,0:T(8,128)(2,1)S(1)}, u32[]{:S(2)}, u32[]{:S(2)}) %collective-permute-start.5) | collective-permute-done | bytes 262176 | tf_op jit(solution)/shard_map/ppermute | solution.py:201
  17.5 0.9 %broadcast_select_fusion.4 = (bf16[8,128,128]{2,1,0:T(8,128)(2,1)}, bf16[8,128,128]{2,1,0:T(8,128)(2,1)}) fusion(bf16[8,128,128]{2,1,0:T(8,128)(2,1)S(1)} %get-tuple-element.48, bf16[8,128,128]{2,1,0:T(8,128)(2,1)S(1)} %collective-permute-done.5, pred[128]{0:T(512)(128)(4,1)S(1)} %get-tuple-element.124, bf16[8,128,128]{2,1,0:T(8,128)(2,1)S(1)} %get-tuple-element.47, ...), kind=kLoop, calls=%fused_computation.45 | loop fusion | flops 262144 | bytes 1572992 | tf_op jit(solution)/shard_map/jit(_where)/select_n | solution.py:297
  18.4 0.6 collective-permute-start.9
  18.9 1.5 %collective-permute-start.10 = (bf16[8,128,128]{2,1,0:T(8,128)(2,1)}, bf16[8,128,128]{2,1,0:T(8,128)(2,1)}, u32[]{:S(2)}, u32[]{:S(2)}) collective-permute-start(bf16[8,128,128]{2,1,0:T(8,128)(2,1)} %get-tuple-element.62), channel_id=1, source_target_pairs={{0,16},{4,20},{8,24},{12,28},{16,0},{20,4},{24,8},{28,12},{1,17},{... | collective-permute-start | bytes 786440 | tf_op jit(solution)/shard_map/ppermute | solution.py:201
  20.5 0.6 collective-permute-done.8
  21.1 2.0 %collective-permute-done.7 = bf16[8,128,128]{2,1,0:T(8,128)(2,1)S(1)} collective-permute-done((bf16[8,128,128]{2,1,0:T(8,128)(2,1)S(1)}, bf16[8,128,128]{2,1,0:T(8,128)(2,1)S(1)}, u32[]{:S(2)}, u32[]{:S(2)}) %collective-permute-start.7) | collective-permute-done | bytes 262176 | tf_op jit(solution)/shard_map/ppermute | solution.py:201
  23.1 1.0 %fusion.5 = (bf16[8,128,128]{2,1,0:T(8,128)(2,1)S(1)}, bf16[8,128,128]{2,1,0:T(8,128)(2,1)S(1)}, bf16[8,128,128]{2,1,0:T(8,128)(2,1)}, bf16[8,128,128]{2,1,0:T(8,128)(2,1)}) fusion(bf16[8,128,128]{2,1,0:T(8,128)(2,1)S(1)} %collective-permute-done.8, bf16[8,128,128]{2,1,0:T(8,128)(2,1)S(1)} %collective-permute-done.5, ...), kind=kLoop, calls=%fused_computation.19 | loop fusion | flops 1048576 | bytes 3670536 | tf_op jit(solution)/shard_map/jit(_where)/select_n | solution.py:303
  24.1 5.7 %round_coeffs.3 = f32[8,1536]{1,0:T(8,128)S(1)} custom-call(s32[1536]{0:T(1024)S(1)} %get-tuple-element.54.index_ref, bf16[8,128,128]{2,1,0:T(8,128)(2,1)S(1)} %get-tuple-element.84.va_ref, bf16[8,128,128]{2,1,0:T(8,128)(2,1)S(1)} %get-tuple-element.83.vb_ref, bf16[3,16,128,128]{3,2,1,0:T(8,128)(2,1)S(1)} %get-tuple-element.57.c0_ref, ...), custom_call_target="tpu_custom_call" | custom-call | flops 4000000000 | bytes 12582912 | tf_op jit(solution)/shard_map/round_coeffs/pallas_call | solution.py:86
  29.8 0.6 fusion.43
  32.3 0.2 conditional.1
  32.6 1.5 %fusion.19 = (bf16[8,128,128]{2,1,0:T(8,128)(2,1)S(1)}, bf16[8,128,128]{2,1,0:T(8,128)(2,1)S(1)}) fusion(bf16[8,128,128]{2,1,0:T(8,128)(2,1)} %get-tuple-element.64, bf16[8,128,128]{2,1,0:T(8,128)(2,1)} %collective-permute-done.10, bf16[8,128,128]{2,1,0:T(8,128)(2,1)} %copy-done.8, bf16[8,128,128]{2,1,0:T(8,128)(2,1)} %copy-done.11, ...), kind=kLoop, calls=%fused_computation.38 | loop fusion | flops 1310720 | bytes 2098436 | tf_op jit(solution)/shard_map/jit(_where)/select_n | solution.py:317
  34.1 1.2 %fusion.9 = (bf16[8,128,128]{2,1,0:T(8,128)(2,1)S(1)}, bf16[8,128,128]{2,1,0:T(8,128)(2,1)S(1)}) fusion(bf16[8,128,128]{2,1,0:T(8,128)(2,1)S(1)} %copy-done.12, bf16[8,128,128]{2,1,0:T(8,128)(2,1)} %collective-permute-done.9, bf16[8,128,128]{2,1,0:T(8,128)(2,1)S(1)} %copy-done.10, bf16[8,128,128]{2,1,0:T(8,128)(2,1)S(1)} %copy-done.7, ...), kind=kLoop, calls=%fused_computation.23 | loop fusion | flops 1310720 | bytes 2098436 | tf_op jit(solution)/shard_map/jit(_where)/select_n | solution.py:318
  35.4 5.6 %round_coeffs.5 = f32[8,1536]{1,0:T(8,128)S(1)} custom-call(s32[1536]{0:T(1024)S(1)} %get-tuple-element.54.index_ref, bf16[8,128,128]{2,1,0:T(8,128)(2,1)S(1)} %get-tuple-element.78.va_ref, bf16[8,128,128]{2,1,0:T(8,128)(2,1)S(1)} %get-tuple-element.76.vb_ref, bf16[3,16,128,128]{3,2,1,0:T(8,128)(2,1)S(1)} %get-tuple-element.57.c0_ref, ...), custom_call_target="tpu_custom_call" | custom-call | flops 4000000000 | bytes 12582912 | tf_op jit(solution)/shard_map/round_coeffs/pallas_call | solution.py:86
  41.0 5.6 %round_coeffs.4 = f32[8,1536]{1,0:T(8,128)S(1)} custom-call(s32[1536]{0:T(1024)S(1)} %get-tuple-element.54.index_ref, bf16[8,128,128]{2,1,0:T(8,128)(2,1)S(1)} %get-tuple-element.77.va_ref, bf16[8,128,128]{2,1,0:T(8,128)(2,1)S(1)} %get-tuple-element.75.vb_ref, bf16[3,16,128,128]{3,2,1,0:T(8,128)(2,1)S(1)} %get-tuple-element.57.c0_ref, ...), custom_call_target="tpu_custom_call" | custom-call | flops 4000000000 | bytes 12582912 | tf_op jit(solution)/shard_map/round_coeffs/pallas_call | solution.py:86
  46.8 0.1 collective-permute-start.11
  46.9 1.3 %collective-permute-done.11 = f32[9,1536]{1,0:T(8,128)S(1)} collective-permute-done((f32[9,1536]{1,0:T(8,128)S(1)}, f32[9,1536]{1,0:T(8,128)S(1)}, u32[]{:S(2)}, u32[]{:S(2)}) %collective-permute-start.11) | collective-permute-done | bytes 55328 | tf_op jit(solution)/shard_map/ppermute | solution.py:201
  48.1 0.1 fusion.39
  48.2 3.7 %collective-permute-start.14 = (bf16[9,1536]{1,0:T(8,128)(2,1)S(1)}, bf16[9,1536]{1,0:T(8,128)(2,1)S(1)}, u32[]{:S(2)}, u32[]{:S(2)}) collective-permute-start(bf16[9,1536]{1,0:T(8,128)(2,1)S(1)} %fusion.39), channel_id=1, source_target_pairs={{0,3},{1,0},{2,1},{3,2},{4,7},{5,4},{6,5},{7,6},{8,11},{9,8},{10,9... | collective-permute-start | bytes 82952 | tf_op jit(solution)/shard_map/ppermute | solution.py:334
  51.9 1.0 %collective-permute-start.12 = (bf16[9,1536]{1,0:T(8,128)(2,1)S(1)}, bf16[9,1536]{1,0:T(8,128)(2,1)S(1)}, u32[]{:S(2)}, u32[]{:S(2)}) collective-permute-start(bf16[9,1536]{1,0:T(8,128)(2,1)S(1)} %fusion.39), channel_id=1, source_target_pairs={{0,1},{1,2},{2,3},{3,0},{4,5},{5,6},{6,7},{7,4},{8,9},{9,10},{10,1... | collective-permute-start | bytes 82952 | tf_op jit(solution)/shard_map/ppermute | solution.py:334
  52.9 0.1 slice_reduce_fusion
  53.0 0.9 %collective-permute-done.14 = bf16[9,1536]{1,0:T(8,128)(2,1)S(1)} collective-permute-done((bf16[9,1536]{1,0:T(8,128)(2,1)S(1)}, bf16[9,1536]{1,0:T(8,128)(2,1)S(1)}, u32[]{:S(2)}, u32[]{:S(2)}) %collective-permute-start.14) | collective-permute-done | bytes 27680 | tf_op jit(solution)/shard_map/ppermute | solution.py:334
  54.0 3.2 %collective-permute-done.13 = bf16[9,1536]{1,0:T(8,128)(2,1)S(1)} collective-permute-done((bf16[9,1536]{1,0:T(8,128)(2,1)S(1)}, bf16[9,1536]{1,0:T(8,128)(2,1)S(1)}, u32[]{:S(2)}, u32[]{:S(2)}) %collective-permute-start.13) | collective-permute-done | bytes 27680 | tf_op jit(solution)/shard_map/ppermute | solution.py:334
  57.2 0.6 collective-permute-done.12
  57.8 0.1 multiply_convert_fusion
  57.9 1.5 %collective-permute-start.17 = (bf16[9,768]{1,0:T(8,128)(2,1)S(1)}, bf16[9,768]{1,0:T(8,128)(2,1)S(1)}, u32[]{:S(2)}, u32[]{:S(2)}) collective-permute-start(bf16[9,768]{1,0:T(8,128)(2,1)S(1)} %get-tuple-element.129), channel_id=1, source_target_pairs={{0,24},{4,28},{8,16},{12,20},{16,8},{20,12},{24,0},{28,4},{1,25},{... | collective-permute-start | bytes 41480 | tf_op jit(solution)/shard_map/ppermute | solution.py:201
  59.4 0.5 collective-permute-start.16
  59.9 1.5 %collective-permute-start.15 = (bf16[9,768]{1,0:T(8,128)(2,1)S(1)}, bf16[9,768]{1,0:T(8,128)(2,1)S(1)}, u32[]{:S(2)}, u32[]{:S(2)}) collective-permute-start(bf16[9,768]{1,0:T(8,128)(2,1)S(1)} %get-tuple-element.127), channel_id=1, source_target_pairs={{0,8},{4,12},{8,0},{12,4},{16,24},{20,28},{24,16},{28,20},{1,9},{5... | collective-permute-start | bytes 41480 | tf_op jit(solution)/shard_map/ppermute | solution.py:201
  61.5 1.2 %collective-permute-done.17 = bf16[9,768]{1,0:T(8,128)(2,1)S(1)} collective-permute-done((bf16[9,768]{1,0:T(8,128)(2,1)S(1)}, bf16[9,768]{1,0:T(8,128)(2,1)S(1)}, u32[]{:S(2)}, u32[]{:S(2)}) %collective-permute-start.17) | collective-permute-done | bytes 13856 | tf_op jit(solution)/shard_map/ppermute | solution.py:201
  62.7 0.5 collective-permute-done.16
  63.3 0.5 collective-permute-done.15
  63.8 0.1 broadcast_select_fusion.7
  63.9 0.1 collective-permute-start.18
  64.0 1.2 %collective-permute-done.18 = bf16[36,576]{1,0:T(8,128)(2,1)S(1)} collective-permute-done((bf16[36,576]{1,0:T(8,128)(2,1)S(1)}, bf16[36,576]{1,0:T(8,128)(2,1)S(1)}, u32[]{:S(2)}, u32[]{:S(2)}) %collective-permute-start.18) | collective-permute-done | bytes 41504 | tf_op jit(solution)/shard_map/ppermute | solution.py:201
  65.2 0.9 %fusion = f32[192,384]{1,0:T(8,128)} fusion(bf16[36,384]{1,0:T(8,128)(2,1)S(1)} %slice.171, bf16[36,384]{1,0:T(8,128)(2,1)S(1)} %slice.169, bf16[36,192]{1,0:T(8,128)(2,1)S(1)} %slice.170, bf16[36,192]{1,0:T(8,128)(2,1)S(1)} %get-tuple-element.91), kind=kOutput, calls=%fused_computation.8 | convolution fusion | flops 10930176 | bytes 377856 | tf_op jit(solution)/shard_map/dot_general | solution.py:356
  (56 shorter events, 0.5 us)
Async XLA Ops:
  1.1 2.0 %collective-permute-start.2 = (bf16[1,8,128,128]{3,2,1,0:T(8,128)(2,1)S(1)}, bf16[1,8,128,128]{3,2,1,0:T(8,128)(2,1)S(1)}, u32[]{:S(2)}, u32[]{:S(2)}) collective-permute-start(bf16[1,8,128,128]{3,2,1,0:T(8,128)(2,1)S(1)} %get-tuple-element.88), channel_id=1, source_target_pairs={{0,4},{4,0},{8,12},{12,8},{16,20},{20,16},{24,28},{28,24},{1,5},{5... | collective-permute-start | bytes 786440 | tf_op jit(solution)/shard_map/ppermute | solution.py:201
  1.6 1.5 %collective-permute-start.3 = (bf16[1,8,128,128]{3,2,1,0:T(8,128)(2,1)S(1)}, bf16[1,8,128,128]{3,2,1,0:T(8,128)(2,1)S(1)}, u32[]{:S(2)}, u32[]{:S(2)}) collective-permute-start(bf16[1,8,128,128]{3,2,1,0:T(8,128)(2,1)S(1)} %get-tuple-element.87), channel_id=1, source_target_pairs={{0,4},{4,0},{8,12},{12,8},{16,20},{20,16},{24,28},{28,24},{1,5},{5... | collective-permute-start | bytes 786440 | tf_op jit(solution)/shard_map/ppermute | solution.py:201
  3.0 2.5 %copy-start.4 = (bf16[1,8,128,128]{3,2,1,0:T(8,128)(2,1)}, bf16[1,8,128,128]{3,2,1,0:T(8,128)(2,1)S(1)}, u32[]{:S(2)}) copy-start(bf16[1,8,128,128]{3,2,1,0:T(8,128)(2,1)S(1)} %collective-permute-done.2) | copy-start | bytes 786436
  3.1 2.4 %copy-start.14 = (s32[32,128]{1,0:T(8,128)S(1)}, s32[32,128]{1,0:T(8,128)}, u32[]{:S(2)}) copy-start(s32[32,128]{1,0:T(8,128)} %get-tuple-element.53) | copy-start | bytes 49156
  3.1 2.4 %copy-start.2 = (bf16[1,32,128,128]{3,2,1,0:T(8,128)(2,1)S(1)}, bf16[1,32,128,128]{3,2,1,0:T(8,128)(2,1)}, u32[]{:S(2)}) copy-start(bf16[1,32,128,128]{3,2,1,0:T(8,128)(2,1)} %param.8) | copy-start | bytes 3145732
  4.7 5.7 %copy-start.13 = (s32[3,1536]{1,0:T(4,128)S(1)}, s32[3,1536]{1,0:T(4,128)}, u32[]{:S(2)}) copy-start(s32[3,1536]{1,0:T(4,128)} %param.12) | copy-start | bytes 55300
  4.7 8.9 %collective-permute-start.6 = (bf16[3,16,128,128]{3,2,1,0:T(8,128)(2,1)S(1)}, bf16[3,16,128,128]{3,2,1,0:T(8,128)(2,1)}, u32[]{:S(2)}, u32[]{:S(2)}) collective-permute-start(bf16[3,16,128,128]{3,2,1,0:T(8,128)(2,1)S(1)} %constant_dynamic-slice_fusion.4), channel_id=1, source_target_pairs={{0,4},{4,0},{8,12},{12,8},{16,20},{20,16},{24,28},{28,24},{1,5},{5... | collective-permute-start | bytes 4718600 | tf_op jit(solution)/shard_map/ppermute | solution.py:201
  5.6 10.4 %collective-permute-start.4 = (bf16[8,128,128]{2,1,0:T(8,128)(2,1)S(1)}, bf16[8,128,128]{2,1,0:T(8,128)(2,1)S(1)}, u32[]{:S(2)}, u32[]{:S(2)}) collective-permute-start(bf16[8,128,128]{2,1,0:T(8,128)(2,1)S(1)} %get-tuple-element.47), channel_id=1, source_target_pairs={{0,8},{4,12},{8,0},{12,4},{16,24},{20,28},{24,16},{28,20},{1,9},{5... | collective-permute-start | bytes 786440 | tf_op jit(solution)/shard_map/ppermute | solution.py:201
  8.3 9.2 %collective-permute-start.5 = (bf16[8,128,128]{2,1,0:T(8,128)(2,1)S(1)}, bf16[8,128,128]{2,1,0:T(8,128)(2,1)S(1)}, u32[]{:S(2)}, u32[]{:S(2)}) collective-permute-start(bf16[8,128,128]{2,1,0:T(8,128)(2,1)S(1)} %get-tuple-element.48), channel_id=1, source_target_pairs={{0,16},{4,20},{8,24},{12,28},{16,0},{20,4},{24,8},{28,12},{1,17},{... | collective-permute-start | bytes 786440 | tf_op jit(solution)/shard_map/ppermute | solution.py:201
  9.9 11.2 %collective-permute-start.8 = (bf16[8,128,128]{2,1,0:T(8,128)(2,1)S(1)}, bf16[8,128,128]{2,1,0:T(8,128)(2,1)S(1)}, u32[]{:S(2)}, u32[]{:S(2)}) collective-permute-start(bf16[8,128,128]{2,1,0:T(8,128)(2,1)S(1)} %get-tuple-element.56), channel_id=1, source_target_pairs={{0,8},{4,12},{8,0},{12,4},{16,24},{20,28},{24,16},{28,20},{1,9},{5... | collective-permute-start | bytes 786440 | tf_op jit(solution)/shard_map/ppermute | solution.py:201
  10.4 12.7 %collective-permute-start.7 = (bf16[8,128,128]{2,1,0:T(8,128)(2,1)S(1)}, bf16[8,128,128]{2,1,0:T(8,128)(2,1)S(1)}, u32[]{:S(2)}, u32[]{:S(2)}) collective-permute-start(bf16[8,128,128]{2,1,0:T(8,128)(2,1)S(1)} %get-tuple-element.55), channel_id=1, source_target_pairs={{0,16},{4,20},{8,24},{12,28},{16,0},{20,4},{24,8},{28,12},{1,17},{... | collective-permute-start | bytes 786440 | tf_op jit(solution)/shard_map/ppermute | solution.py:201
  13.6 10.5 %copy-start = (f32[1536,128]{1,0:T(8,128)}, f32[1536,128]{1,0:T(8,128)S(1)}, u32[]{:S(2)}) copy-start(f32[1536,128]{1,0:T(8,128)S(1)} %add_multiply_fusion.tx_ref) | copy-start | bytes 2359300
  16.0 7.1 %copy-start.3 = (bf16[1,32,128,128]{3,2,1,0:T(8,128)(2,1)S(1)}, bf16[1,32,128,128]{3,2,1,0:T(8,128)(2,1)}, u32[]{:S(2)}) copy-start(bf16[1,32,128,128]{3,2,1,0:T(8,128)(2,1)} %param.8) | copy-start | bytes 3145732
  16.1 7.1 %copy-start.5 = (bf16[1,8,128,128]{3,2,1,0:T(8,128)(2,1)S(1)}, bf16[1,8,128,128]{3,2,1,0:T(8,128)(2,1)}, u32[]{:S(2)}) copy-start(bf16[1,8,128,128]{3,2,1,0:T(8,128)(2,1)} %copy-done.4) | copy-start | bytes 786436
  16.1 8.0 %copy-start.8 = (bf16[8,128,128]{2,1,0:T(8,128)(2,1)}, bf16[8,128,128]{2,1,0:T(8,128)(2,1)S(1)}, u32[]{:S(2)}) copy-start(bf16[8,128,128]{2,1,0:T(8,128)(2,1)S(1)} %collective-permute-done.4) | copy-start | bytes 786436
  17.5 6.6 %copy-start.6 = (bf16[8,128,128]{2,1,0:T(8,128)(2,1)}, bf16[8,128,128]{2,1,0:T(8,128)(2,1)S(1)}, u32[]{:S(2)}) copy-start(bf16[8,128,128]{2,1,0:T(8,128)(2,1)S(1)} %collective-permute-done.5) | copy-start | bytes 786436
  18.4 14.2 %collective-permute-start.9 = (bf16[8,128,128]{2,1,0:T(8,128)(2,1)}, bf16[8,128,128]{2,1,0:T(8,128)(2,1)}, u32[]{:S(2)}, u32[]{:S(2)}) collective-permute-start(bf16[8,128,128]{2,1,0:T(8,128)(2,1)} %get-tuple-element.61), channel_id=1, source_target_pairs={{0,8},{4,12},{8,0},{12,4},{16,24},{20,28},{24,16},{28,20},{1,9},{5... | collective-permute-start | bytes 786440 | tf_op jit(solution)/shard_map/ppermute | solution.py:201
  18.9 13.6 %collective-permute-start.10 = (bf16[8,128,128]{2,1,0:T(8,128)(2,1)}, bf16[8,128,128]{2,1,0:T(8,128)(2,1)}, u32[]{:S(2)}, u32[]{:S(2)}) collective-permute-start(bf16[8,128,128]{2,1,0:T(8,128)(2,1)} %get-tuple-element.62), channel_id=1, source_target_pairs={{0,16},{4,20},{8,24},{12,28},{16,0},{20,4},{24,8},{28,12},{1,17},{... | collective-permute-start | bytes 786440 | tf_op jit(solution)/shard_map/ppermute | solution.py:201
  21.1 3.0 %copy-start.9 = (bf16[8,128,128]{2,1,0:T(8,128)(2,1)}, bf16[8,128,128]{2,1,0:T(8,128)(2,1)S(1)}, u32[]{:S(2)}) copy-start(bf16[8,128,128]{2,1,0:T(8,128)(2,1)S(1)} %collective-permute-done.8) | copy-start | bytes 786436
  23.1 1.0 %copy-start.11 = (bf16[8,128,128]{2,1,0:T(8,128)(2,1)}, bf16[8,128,128]{2,1,0:T(8,128)(2,1)S(1)}, u32[]{:S(2)}) copy-start(bf16[8,128,128]{2,1,0:T(8,128)(2,1)S(1)} %collective-permute-done.7) | copy-start | bytes 786436
  32.5 1.6 %copy-start.7 = (bf16[8,128,128]{2,1,0:T(8,128)(2,1)S(1)}, bf16[8,128,128]{2,1,0:T(8,128)(2,1)}, u32[]{:S(2)}) copy-start(bf16[8,128,128]{2,1,0:T(8,128)(2,1)} %copy-done.6) | copy-start | bytes 786436
  32.5 1.6 %copy-start.10 = (bf16[8,128,128]{2,1,0:T(8,128)(2,1)S(1)}, bf16[8,128,128]{2,1,0:T(8,128)(2,1)}, u32[]{:S(2)}) copy-start(bf16[8,128,128]{2,1,0:T(8,128)(2,1)} %copy-done.9) | copy-start | bytes 786436
  32.5 1.6 %copy-start.12 = (bf16[8,128,128]{2,1,0:T(8,128)(2,1)S(1)}, bf16[8,128,128]{2,1,0:T(8,128)(2,1)}, u32[]{:S(2)}) copy-start(bf16[8,128,128]{2,1,0:T(8,128)(2,1)} %get-tuple-element.66) | copy-start | bytes 786436
  34.1 1.3 %copy-start.1 = (f32[1536,128]{1,0:T(8,128)S(1)}, f32[1536,128]{1,0:T(8,128)}, u32[]{:S(2)}) copy-start(f32[1536,128]{1,0:T(8,128)} %copy-done) | copy-start | bytes 2359300
  41.0 11.9 %copy-start.15 = (f32[16,128]{1,0:T(8,128)S(1)}, f32[16,128]{1,0:T(8,128)}, u32[]{:S(2)}) copy-start(f32[16,128]{1,0:T(8,128)} %get-tuple-element.68) | copy-start | bytes 24580
  46.8 1.4 %collective-permute-start.11 = (f32[9,1536]{1,0:T(8,128)S(1)}, f32[9,1536]{1,0:T(8,128)S(1)}, u32[]{:S(2)}, u32[]{:S(2)}) collective-permute-start(f32[9,1536]{1,0:T(8,128)S(1)} %fusion.24), channel_id=1, source_target_pairs={{0,4},{4,0},{8,12},{12,8},{16,20},{20,16},{24,28},{28,24},{1,5},{5... | collective-permute-start | bytes 165896 | tf_op jit(solution)/shard_map/ppermute | solution.py:201
  48.2 5.8 %collective-permute-start.14 = (bf16[9,1536]{1,0:T(8,128)(2,1)S(1)}, bf16[9,1536]{1,0:T(8,128)(2,1)S(1)}, u32[]{:S(2)}, u32[]{:S(2)}) collective-permute-start(bf16[9,1536]{1,0:T(8,128)(2,1)S(1)} %fusion.39), channel_id=1, source_target_pairs={{0,3},{1,0},{2,1},{3,2},{4,7},{5,4},{6,5},{7,6},{8,11},{9,8},{10,9... | collective-permute-start | bytes 82952 | tf_op jit(solution)/shard_map/ppermute | solution.py:334
  51.9 5.3 %collective-permute-start.13 = (bf16[9,1536]{1,0:T(8,128)(2,1)S(1)}, bf16[9,1536]{1,0:T(8,128)(2,1)S(1)}, u32[]{:S(2)}, u32[]{:S(2)}) collective-permute-start(bf16[9,1536]{1,0:T(8,128)(2,1)S(1)} %fusion.39), channel_id=1, source_target_pairs={{0,2},{1,3},{2,0},{3,1},{4,6},{5,7},{6,4},{7,5},{8,10},{9,11},{10,... | collective-permute-start | bytes 82952 | tf_op jit(solution)/shard_map/ppermute | solution.py:334
  51.9 5.9 %collective-permute-start.12 = (bf16[9,1536]{1,0:T(8,128)(2,1)S(1)}, bf16[9,1536]{1,0:T(8,128)(2,1)S(1)}, u32[]{:S(2)}, u32[]{:S(2)}) collective-permute-start(bf16[9,1536]{1,0:T(8,128)(2,1)S(1)} %fusion.39), channel_id=1, source_target_pairs={{0,1},{1,2},{2,3},{3,0},{4,5},{5,6},{6,7},{7,4},{8,9},{9,10},{10,1... | collective-permute-start | bytes 82952 | tf_op jit(solution)/shard_map/ppermute | solution.py:334
  57.9 4.8 %collective-permute-start.17 = (bf16[9,768]{1,0:T(8,128)(2,1)S(1)}, bf16[9,768]{1,0:T(8,128)(2,1)S(1)}, u32[]{:S(2)}, u32[]{:S(2)}) collective-permute-start(bf16[9,768]{1,0:T(8,128)(2,1)S(1)} %get-tuple-element.129), channel_id=1, source_target_pairs={{0,24},{4,28},{8,16},{12,20},{16,8},{20,12},{24,0},{28,4},{1,25},{... | collective-permute-start | bytes 41480 | tf_op jit(solution)/shard_map/ppermute | solution.py:201
  59.4 3.8 %collective-permute-start.16 = (bf16[9,768]{1,0:T(8,128)(2,1)S(1)}, bf16[9,768]{1,0:T(8,128)(2,1)S(1)}, u32[]{:S(2)}, u32[]{:S(2)}) collective-permute-start(bf16[9,768]{1,0:T(8,128)(2,1)S(1)} %get-tuple-element.128), channel_id=1, source_target_pairs={{0,16},{4,20},{8,24},{12,28},{16,0},{20,4},{24,8},{28,12},{1,17},{... | collective-permute-start | bytes 41480 | tf_op jit(solution)/shard_map/ppermute | solution.py:201
  59.9 3.8 %collective-permute-start.15 = (bf16[9,768]{1,0:T(8,128)(2,1)S(1)}, bf16[9,768]{1,0:T(8,128)(2,1)S(1)}, u32[]{:S(2)}, u32[]{:S(2)}) collective-permute-start(bf16[9,768]{1,0:T(8,128)(2,1)S(1)} %get-tuple-element.127), channel_id=1, source_target_pairs={{0,8},{4,12},{8,0},{12,4},{16,24},{20,28},{24,16},{28,20},{1,9},{5... | collective-permute-start | bytes 41480 | tf_op jit(solution)/shard_map/ppermute | solution.py:201
  63.9 1.3 %collective-permute-start.18 = (bf16[36,576]{1,0:T(8,128)(2,1)S(1)}, bf16[36,576]{1,0:T(8,128)(2,1)S(1)}, u32[]{:S(2)}, u32[]{:S(2)}) collective-permute-start(bf16[36,576]{1,0:T(8,128)(2,1)S(1)} %pad_maximum_fusion.3), channel_id=1, source_target_pairs={{0,4},{4,0},{8,12},{12,8},{16,20},{20,16},{24,28},{28,24},{1,5},{5... | collective-permute-start | bytes 124424 | tf_op jit(solution)/shard_map/ppermute | solution.py:201
where the time goes:
time: 66.4 us; the launch traced here: 66.2 us
  Pallas kernels  18.3 us (28%)
  starting transfers between devices  16.3 us (25%)
  waiting for transfers between devices  13.6 us (20%)
  other arithmetic  10.9 us (16%)
  local copies, waits for them, and re-layouts  3.59 us (5%)
  between operations  2.26 us (3%)
  matrix products  0.94 us (1%)
    pallas_call x3, Pallas kernels, round_coeffs(): pl.pallas_call(round_kernel, out_shape=jax.ShapeDtypeStruct((rows, keep),...  16.9 us
    ppermute x14, starting transfers between devices, swap(): return lax.ppermute(value, 'band', [(i, i ^ mask) for i in range(n_band)])  11.6 us
    ppermute x14, waiting for transfers between devices, swap(): return lax.ppermute(value, 'band', [(i, i ^ mask) for i in range(n_band)])  8.9 us
    ppermute x3, waiting for transfers between devices, per_device(): lax.ppermute(sent, 'col', [(i, (i + shift) % n_col) for i in range(n_col)])  4.72 us
    ppermute x3, starting transfers between devices, per_device(): lax.ppermute(sent, 'col', [(i, (i + shift) % n_col) for i in range(n_col)])  4.67 us
    mul x1, other arithmetic, prepared(): cas_of(kept[0][:, None] * x_global[None, :] % length, length)  3.17 us
    select_n x1, other arithmetic, prepared(): c1 = jnp.where(side == 0, c_swapped, c_mine)  2.38 us
    dynamic_slice x1, local copies, waits for them, and re-layouts, half_of(): return lax.dynamic_slice_in_dim(value, which * x_half, x_half, 1)  1.6 us
  transfers between devices with their start and end apart: 17, of which 12 were waited for; matrix products, arithmetic and copies ran while one was open for 13% of the time, Pallas kernels for 11%

commit v1 on v0

--- a/solution.py
+++ b/solution.py
@@ -293,7 +293,8 @@
         x_a, y_b = swap(to_x[0], 2), swap(to_y[1], 4)
         x_b, y_a = swap(to_x[1], 2), swap(to_y[0], 4)
         ready = prepared(*given)
-        x_a, y_b, ready = lax.optimization_barrier((x_a, y_b, ready))
+        again = (flags[3, 0] != 0).astype(jnp.int32)
+        x_a, y_b, ready, again = lax.optimization_barrier((x_a, y_b, ready, again))
         on_y, on_x = jnp.where(flag(0), to_x[0], x_a), jnp.where(flag(0), to_y[1], y_b)
         on_y, on_x, flags = lax.optimization_barrier((on_y, on_x, flags))
         on_y, on_x = swap(on_y, 4), swap(on_x, 2)
@@ -306,7 +307,7 @@
         partial, on_x, on_y = lax.optimization_barrier((partial, on_x, on_y))
         later_x, later_y = jnp.where(flag(0), to_y[0], y_a), jnp.where(flag(0), to_x[1], x_b)
         last_x, last_y = lax.cond(
-            flags[3, 0] != 0,
+            again != 0,
             lambda x, y: (swap(x, 2), swap(y, 4)),
             lambda x, y: (x, y),
             later_x,

time: 66.4 us -> 66.4 us (level)
  waiting for transfers between devices: 13.6 us -> 12.4 us
  starting transfers between devices: 16.3 us -> 17 us
    ppermute x14, waiting for transfers between devices: 8.9 us -> 7.72 us  [swap(): return lax.ppermute(value, 'band', [(i, i ^ mask) for i in range(n_band)])]
    ppermute x14, starting transfers between devices: 11.6 us -> 12.3 us  [swap(): return lax.ppermute(value, 'band', [(i, i ^ mask) for i in range(n_band)])]
  transfers between devices with their start and end apart: 17 -> 17, of which waited for: 12 -> 11; matrix products, arithmetic and copies ran while one was open for 13% -> 14% of each run, Pallas kernels for 11% -> 11%
where the time goes in v1:
time: 66.4 us; the launch traced here: 66.1 us
  Pallas kernels  18.3 us (28%)
  starting transfers between devices  17 us (26%)
  waiting for transfers between devices  12.4 us (19%)
  other arithmetic  10.9 us (16%)
  local copies, waits for them, and re-layouts  4.1 us (6%)
  between operations  2.22 us (3%)
  matrix products  0.94 us (1%)
    pallas_call x3, Pallas kernels, round_coeffs(): pl.pallas_call(round_kernel, out_shape=jax.ShapeDtypeStruct((rows, keep),...  17 us
    ppermute x14, starting transfers between devices, swap(): return lax.ppermute(value, 'band', [(i, i ^ mask) for i in range(n_band)])  12.3 us
    ppermute x14, waiting for transfers between devices, swap(): return lax.ppermute(value, 'band', [(i, i ^ mask) for i in range(n_band)])  7.72 us
    ppermute x3, waiting for transfers between devices, per_device(): lax.ppermute(sent, 'col', [(i, (i + shift) % n_col) for i in range(n_col)])  4.72 us
    ppermute x3, starting transfers between devices, per_device(): lax.ppermute(sent, 'col', [(i, (i + shift) % n_col) for i in range(n_col)])  4.64 us
    mul x1, other arithmetic, prepared(): cas_of(kept[0][:, None] * x_global[None, :] % length, length)  3.17 us
    select_n x1, other arithmetic, prepared(): c1 = jnp.where(side == 0, c_swapped, c_mine)  2.38 us
    dynamic_slice x1, local copies, waits for them, and re-layouts, half_of(): return lax.dynamic_slice_in_dim(value, which * x_half, x_half, 1)  1.6 us
  transfers between devices with their start and end apart: 17, of which 11 were waited for; matrix products, arithmetic and copies ran while one was open for 14% of the time, Pallas kernels for 11%

profile of v1, /device:TPU:0, one launch (start us, length us, event | category | flops | bytes accessed | tf_op | source)
XLA Modules:
  0.0 66.1 jit_solution(14285236459595119203)
XLA Ops:
  0.0 1.1 %constant_dynamic-slice_fusion.5 = (bf16[1,8,128,128]{3,2,1,0:T(8,128)(2,1)S(1)}, bf16[1,8,128,128]{3,2,1,0:T(8,128)(2,1)S(1)}) fusion(bf16[1,32,128,128]{3,2,1,0:T(8,128)(2,1)} %param.8, s32[]{:T(128)S(6)} %select_n.212, s32[]{:T(128)S(6)} %select_n.211), kind=kLoop, calls=%fused_computation.86 | loop fusion | bytes 1048584 | tf_op jit(solution)/shard_map/dynamic_slice | solution.py:210
  1.1 0.5 collective-permute-start.2
  1.6 0.1 collective-permute-start.3
  1.7 1.4 %square_flags.1 = (s32[32,128]{1,0:T(8,128)}, f32[16,128]{1,0:T(8,128)}) custom-call(s32[3]{0:T(128)} %plan_ref.1, f32[8]{0:T(128)} %energy_val_ref.1, f32[3]{0:T(128)} %energy_cond_ref.1), custom_call_target="tpu_custom_call" | custom-call | tf_op jit(solution)/shard_map/square_flags/pallas_call | solution.py:174
  3.0 0.1 collective-permute-done.3
  3.1 1.6 %constant_dynamic-slice_fusion.4 = bf16[3,16,128,128]{3,2,1,0:T(8,128)(2,1)S(1)} fusion(bf16[3,32,128,128]{3,2,1,0:T(8,128)(2,1)} %param.9, s32[]{:T(128)S(6)} %select_n.211), kind=kLoop, calls=%fused_computation.85 | loop fusion | bytes 3145732 | tf_op jit(solution)/shard_map/dynamic_slice | solution.py:204
  4.7 0.5 collective-permute-start.6
  5.2 0.3 add_convert_fusion.table_ref
  5.5 0.5 slice.130
  6.0 0.1 bitcast_select_fusion.8
  6.1 2.7 %collective-permute-start.4 = (bf16[8,128,128]{2,1,0:T(8,128)(2,1)S(1)}, bf16[8,128,128]{2,1,0:T(8,128)(2,1)S(1)}, u32[]{:S(2)}, u32[]{:S(2)}) collective-permute-start(bf16[8,128,128]{2,1,0:T(8,128)(2,1)S(1)} %get-tuple-element.48), channel_id=1, source_target_pairs={{0,8},{4,12},{8,0},{12,4},{16,24},{20,28},{24,16},{28,20},{1,9},{5... | collective-permute-start | bytes 786440 | tf_op jit(solution)/shard_map/ppermute | solution.py:201
  8.8 1.5 %collective-permute-start.5 = (bf16[8,128,128]{2,1,0:T(8,128)(2,1)S(1)}, bf16[8,128,128]{2,1,0:T(8,128)(2,1)S(1)}, u32[]{:S(2)}, u32[]{:S(2)}) collective-permute-start(bf16[8,128,128]{2,1,0:T(8,128)(2,1)S(1)} %get-tuple-element.49), channel_id=1, source_target_pairs={{0,16},{4,20},{8,24},{12,28},{16,0},{20,4},{24,8},{28,12},{1,17},{... | collective-permute-start | bytes 786440 | tf_op jit(solution)/shard_map/ppermute | solution.py:201
  10.9 0.6 collective-permute-start.8
  11.6 3.2 %add_multiply_fusion.tx_ref = f32[1536,128]{1,0:T(8,128)S(1)} fusion(s32[128]{0:T(128)S(1)} %fusion.37, s32[1536]{0:T(1024)S(1)} %get-tuple-element.72), kind=kLoop, calls=%fused_computation.12 | loop fusion | flops 3145728 | bytes 793088 | tf_op jit(solution)/shard_map/mul | solution.py:226
  14.8 2.4 %broadcast_select_fusion = (bf16[3,16,128,128]{3,2,1,0:T(8,128)(2,1)S(1)}, bf16[3,16,128,128]{3,2,1,0:T(8,128)(2,1)S(1)}) fusion(bf16[3,16,128,128]{3,2,1,0:T(8,128)(2,1)} %collective-permute-done.6, pred[]{:T(512)S(6)} %eq.10, bf16[3,32,128,128]{3,2,1,0:T(8,128)(2,1)} %param.9, s32[]{:T(128)S(6)} %select_n.213), kind=kLoop, calls=%fused_computation | loop fusion | flops 1572864 | bytes 6291461 | tf_op jit(solution)/shard_map/jit(_where)/select_n | solution.py:229
  17.2 0.8 %collective-permute-done.5 = bf16[8,128,128]{2,1,0:T(8,128)(2,1)S(1)} collective-permute-done((bf16[8,128,128]{2,1,0:T(8,128)(2,1)S(1)}, bf16[8,128,128]{2,1,0:T(8,128)(2,1)S(1)}, u32[]{:S(2)}, u32[]{:S(2)}) %collective-permute-start.5) | collective-permute-done | bytes 262176 | tf_op jit(solution)/shard_map/ppermute | solution.py:201
  18.0 0.9 %broadcast_select_fusion.4 = (bf16[8,128,128]{2,1,0:T(8,128)(2,1)}, bf16[8,128,128]{2,1,0:T(8,128)(2,1)}) fusion(bf16[8,128,128]{2,1,0:T(8,128)(2,1)S(1)} %get-tuple-element.49, bf16[8,128,128]{2,1,0:T(8,128)(2,1)S(1)} %collective-permute-done.5, pred[128]{0:T(512)(128)(4,1)S(1)} %get-tuple-element.125, bf16[8,128,128]{2,1,0:T(8,128)(2,1)S(1)} %get-tuple-element.48, ...), kind=kLoop, calls=%fused_computation.45 | loop fusion | flops 262144 | bytes 1572992 | tf_op jit(solution)/shard_map/jit(_where)/select_n | solution.py:298
  18.9 1.2 %collective-permute-start.9 = (bf16[8,128,128]{2,1,0:T(8,128)(2,1)}, bf16[8,128,128]{2,1,0:T(8,128)(2,1)}, u32[]{:S(2)}, u32[]{:S(2)}) collective-permute-start(bf16[8,128,128]{2,1,0:T(8,128)(2,1)} %get-tuple-element.62), channel_id=1, source_target_pairs={{0,8},{4,12},{8,0},{12,4},{16,24},{20,28},{24,16},{28,20},{1,9},{5... | collective-permute-start | bytes 786440 | tf_op jit(solution)/shard_map/ppermute | solution.py:201
  20.0 1.5 %collective-permute-start.10 = (bf16[8,128,128]{2,1,0:T(8,128)(2,1)}, bf16[8,128,128]{2,1,0:T(8,128)(2,1)}, u32[]{:S(2)}, u32[]{:S(2)}) collective-permute-start(bf16[8,128,128]{2,1,0:T(8,128)(2,1)} %get-tuple-element.63), channel_id=1, source_target_pairs={{0,16},{4,20},{8,24},{12,28},{16,0},{20,4},{24,8},{28,12},{1,17},{... | collective-permute-start | bytes 786440 | tf_op jit(solution)/shard_map/ppermute | solution.py:201
  21.6 2.0 %collective-permute-done.7 = bf16[8,128,128]{2,1,0:T(8,128)(2,1)S(1)} collective-permute-done((bf16[8,128,128]{2,1,0:T(8,128)(2,1)S(1)}, bf16[8,128,128]{2,1,0:T(8,128)(2,1)S(1)}, u32[]{:S(2)}, u32[]{:S(2)}) %collective-permute-start.7) | collective-permute-done | bytes 262176 | tf_op jit(solution)/shard_map/ppermute | solution.py:201
  23.6 1.0 %fusion.5 = (bf16[8,128,128]{2,1,0:T(8,128)(2,1)S(1)}, bf16[8,128,128]{2,1,0:T(8,128)(2,1)S(1)}, bf16[8,128,128]{2,1,0:T(8,128)(2,1)}, bf16[8,128,128]{2,1,0:T(8,128)(2,1)}) fusion(bf16[8,128,128]{2,1,0:T(8,128)(2,1)S(1)} %collective-permute-done.8, bf16[8,128,128]{2,1,0:T(8,128)(2,1)S(1)} %collective-permute-done.5, ...), kind=kLoop, calls=%fused_computation.19 | loop fusion | flops 1048576 | bytes 3670536 | tf_op jit(solution)/shard_map/jit(_where)/select_n | solution.py:304
  24.6 5.7 %round_coeffs.3 = f32[8,1536]{1,0:T(8,128)S(1)} custom-call(s32[1536]{0:T(1024)S(1)} %get-tuple-element.55.index_ref, bf16[8,128,128]{2,1,0:T(8,128)(2,1)S(1)} %get-tuple-element.86.va_ref, bf16[8,128,128]{2,1,0:T(8,128)(2,1)S(1)} %get-tuple-element.85.vb_ref, bf16[3,16,128,128]{3,2,1,0:T(8,128)(2,1)S(1)} %get-tuple-element.58.c0_ref, ...), custom_call_target="tpu_custom_call" | custom-call | flops 4000000000 | bytes 12582912 | tf_op jit(solution)/shard_map/round_coeffs/pallas_call | solution.py:86
  30.3 0.6 fusion.43
  32.2 0.2 conditional.1
  32.4 1.5 %fusion.19 = (bf16[8,128,128]{2,1,0:T(8,128)(2,1)S(1)}, bf16[8,128,128]{2,1,0:T(8,128)(2,1)S(1)}) fusion(bf16[8,128,128]{2,1,0:T(8,128)(2,1)} %get-tuple-element.66, bf16[8,128,128]{2,1,0:T(8,128)(2,1)} %collective-permute-done.10, bf16[8,128,128]{2,1,0:T(8,128)(2,1)} %copy-done.8, bf16[8,128,128]{2,1,0:T(8,128)(2,1)} %copy-done.11, ...), kind=kLoop, calls=%fused_computation.38 | loop fusion | flops 1310720 | bytes 2098436 | tf_op jit(solution)/shard_map/jit(_where)/select_n | solution.py:318
  34.0 1.2 %fusion.9 = (bf16[8,128,128]{2,1,0:T(8,128)(2,1)S(1)}, bf16[8,128,128]{2,1,0:T(8,128)(2,1)S(1)}) fusion(bf16[8,128,128]{2,1,0:T(8,128)(2,1)S(1)} %copy-done.12, bf16[8,128,128]{2,1,0:T(8,128)(2,1)} %collective-permute-done.9, bf16[8,128,128]{2,1,0:T(8,128)(2,1)S(1)} %copy-done.10, bf16[8,128,128]{2,1,0:T(8,128)(2,1)S(1)} %copy-done.7, ...), kind=kLoop, calls=%fused_computation.23 | loop fusion | flops 1310720 | bytes 2098436 | tf_op jit(solution)/shard_map/jit(_where)/select_n | solution.py:319
  35.2 5.6 %round_coeffs.5 = f32[8,1536]{1,0:T(8,128)S(1)} custom-call(s32[1536]{0:T(1024)S(1)} %get-tuple-element.55.index_ref, bf16[8,128,128]{2,1,0:T(8,128)(2,1)S(1)} %get-tuple-element.80.va_ref, bf16[8,128,128]{2,1,0:T(8,128)(2,1)S(1)} %get-tuple-element.78.vb_ref, bf16[3,16,128,128]{3,2,1,0:T(8,128)(2,1)S(1)} %get-tuple-element.58.c0_ref, ...), custom_call_target="tpu_custom_call" | custom-call | flops 4000000000 | bytes 12582912 | tf_op jit(solution)/shard_map/round_coeffs/pallas_call | solution.py:86
  40.9 5.6 %round_coeffs.4 = f32[8,1536]{1,0:T(8,128)S(1)} custom-call(s32[1536]{0:T(1024)S(1)} %get-tuple-element.55.index_ref, bf16[8,128,128]{2,1,0:T(8,128)(2,1)S(1)} %get-tuple-element.79.va_ref, bf16[8,128,128]{2,1,0:T(8,128)(2,1)S(1)} %get-tuple-element.77.vb_ref, bf16[3,16,128,128]{3,2,1,0:T(8,128)(2,1)S(1)} %get-tuple-element.58.c0_ref, ...), custom_call_target="tpu_custom_call" | custom-call | flops 4000000000 | bytes 12582912 | tf_op jit(solution)/shard_map/round_coeffs/pallas_call | solution.py:86
  46.7 0.1 collective-permute-start.11
  46.8 1.3 %collective-permute-done.11 = f32[9,1536]{1,0:T(8,128)S(1)} collective-permute-done((f32[9,1536]{1,0:T(8,128)S(1)}, f32[9,1536]{1,0:T(8,128)S(1)}, u32[]{:S(2)}, u32[]{:S(2)}) %collective-permute-start.11) | collective-permute-done | bytes 55328 | tf_op jit(solution)/shard_map/ppermute | solution.py:201
  48.1 0.1 fusion.39
  48.1 3.6 %collective-permute-start.14 = (bf16[9,1536]{1,0:T(8,128)(2,1)S(1)}, bf16[9,1536]{1,0:T(8,128)(2,1)S(1)}, u32[]{:S(2)}, u32[]{:S(2)}) collective-permute-start(bf16[9,1536]{1,0:T(8,128)(2,1)S(1)} %fusion.39), channel_id=1, source_target_pairs={{0,3},{1,0},{2,1},{3,2},{4,7},{5,4},{6,5},{7,6},{8,11},{9,8},{10,9... | collective-permute-start | bytes 82952 | tf_op jit(solution)/shard_map/ppermute | solution.py:335
  51.8 1.0 %collective-permute-start.12 = (bf16[9,1536]{1,0:T(8,128)(2,1)S(1)}, bf16[9,1536]{1,0:T(8,128)(2,1)S(1)}, u32[]{:S(2)}, u32[]{:S(2)}) collective-permute-start(bf16[9,1536]{1,0:T(8,128)(2,1)S(1)} %fusion.39), channel_id=1, source_target_pairs={{0,1},{1,2},{2,3},{3,0},{4,5},{5,6},{6,7},{7,4},{8,9},{9,10},{10,1... | collective-permute-start | bytes 82952 | tf_op jit(solution)/shard_map/ppermute | solution.py:335
  52.8 0.1 slice_reduce_fusion
  52.9 0.9 %collective-permute-done.14 = bf16[9,1536]{1,0:T(8,128)(2,1)S(1)} collective-permute-done((bf16[9,1536]{1,0:T(8,128)(2,1)S(1)}, bf16[9,1536]{1,0:T(8,128)(2,1)S(1)}, u32[]{:S(2)}, u32[]{:S(2)}) %collective-permute-start.14) | collective-permute-done | bytes 27680 | tf_op jit(solution)/shard_map/ppermute | solution.py:335
  53.9 3.2 %collective-permute-done.13 = bf16[9,1536]{1,0:T(8,128)(2,1)S(1)} collective-permute-done((bf16[9,1536]{1,0:T(8,128)(2,1)S(1)}, bf16[9,1536]{1,0:T(8,128)(2,1)S(1)}, u32[]{:S(2)}, u32[]{:S(2)}) %collective-permute-start.13) | collective-permute-done | bytes 27680 | tf_op jit(solution)/shard_map/ppermute | solution.py:335
  57.1 0.6 collective-permute-done.12
  57.6 0.1 multiply_convert_fusion
  57.8 1.5 %collective-permute-start.17 = (bf16[9,768]{1,0:T(8,128)(2,1)S(1)}, bf16[9,768]{1,0:T(8,128)(2,1)S(1)}, u32[]{:S(2)}, u32[]{:S(2)}) collective-permute-start(bf16[9,768]{1,0:T(8,128)(2,1)S(1)} %get-tuple-element.130), channel_id=1, source_target_pairs={{0,24},{4,28},{8,16},{12,20},{16,8},{20,12},{24,0},{28,4},{1,25},{... | collective-permute-start | bytes 41480 | tf_op jit(solution)/shard_map/ppermute | solution.py:201
  59.3 0.6 collective-permute-start.16
  59.9 1.5 %collective-permute-start.15 = (bf16[9,768]{1,0:T(8,128)(2,1)S(1)}, bf16[9,768]{1,0:T(8,128)(2,1)S(1)}, u32[]{:S(2)}, u32[]{:S(2)}) collective-permute-start(bf16[9,768]{1,0:T(8,128)(2,1)S(1)} %get-tuple-element.128), channel_id=1, source_target_pairs={{0,8},{4,12},{8,0},{12,4},{16,24},{20,28},{24,16},{28,20},{1,9},{5... | collective-permute-start | bytes 41480 | tf_op jit(solution)/shard_map/ppermute | solution.py:201
  61.3 1.2 %collective-permute-done.17 = bf16[9,768]{1,0:T(8,128)(2,1)S(1)} collective-permute-done((bf16[9,768]{1,0:T(8,128)(2,1)S(1)}, bf16[9,768]{1,0:T(8,128)(2,1)S(1)}, u32[]{:S(2)}, u32[]{:S(2)}) %collective-permute-start.17) | collective-permute-done | bytes 13856 | tf_op jit(solution)/shard_map/ppermute | solution.py:201
  62.6 0.5 collective-permute-done.16
  63.1 0.6 collective-permute-done.15
  63.7 0.1 broadcast_select_fusion.7
  63.9 0.1 collective-permute-start.18
  63.9 1.2 %collective-permute-done.18 = bf16[36,576]{1,0:T(8,128)(2,1)S(1)} collective-permute-done((bf16[36,576]{1,0:T(8,128)(2,1)S(1)}, bf16[36,576]{1,0:T(8,128)(2,1)S(1)}, u32[]{:S(2)}, u32[]{:S(2)}) %collective-permute-start.18) | collective-permute-done | bytes 41504 | tf_op jit(solution)/shard_map/ppermute | solution.py:201
  65.2 0.9 %fusion = f32[192,384]{1,0:T(8,128)} fusion(bf16[36,384]{1,0:T(8,128)(2,1)S(1)} %slice.171, bf16[36,384]{1,0:T(8,128)(2,1)S(1)} %slice.169, bf16[36,192]{1,0:T(8,128)(2,1)S(1)} %slice.170, bf16[36,192]{1,0:T(8,128)(2,1)S(1)} %get-tuple-element.93), kind=kOutput, calls=%fused_computation.8 | convolution fusion | flops 10930176 | bytes 377856 | tf_op jit(solution)/shard_map/dot_general | solution.py:357
  (57 shorter events, 0.5 us)
Async XLA Ops:
  1.1 2.0 %collective-permute-start.2 = (bf16[1,8,128,128]{3,2,1,0:T(8,128)(2,1)S(1)}, bf16[1,8,128,128]{3,2,1,0:T(8,128)(2,1)S(1)}, u32[]{:S(2)}, u32[]{:S(2)}) collective-permute-start(bf16[1,8,128,128]{3,2,1,0:T(8,128)(2,1)S(1)} %get-tuple-element.90), channel_id=1, source_target_pairs={{0,4},{4,0},{8,12},{12,8},{16,20},{20,16},{24,28},{28,24},{1,5},{5... | collective-permute-start | bytes 786440 | tf_op jit(solution)/shard_map/ppermute | solution.py:201
  1.6 1.5 %collective-permute-start.3 = (bf16[1,8,128,128]{3,2,1,0:T(8,128)(2,1)S(1)}, bf16[1,8,128,128]{3,2,1,0:T(8,128)(2,1)S(1)}, u32[]{:S(2)}, u32[]{:S(2)}) collective-permute-start(bf16[1,8,128,128]{3,2,1,0:T(8,128)(2,1)S(1)} %get-tuple-element.89), channel_id=1, source_target_pairs={{0,4},{4,0},{8,12},{12,8},{16,20},{20,16},{24,28},{28,24},{1,5},{5... | collective-permute-start | bytes 786440 | tf_op jit(solution)/shard_map/ppermute | solution.py:201
  3.0 3.0 %copy-start.4 = (bf16[1,8,128,128]{3,2,1,0:T(8,128)(2,1)}, bf16[1,8,128,128]{3,2,1,0:T(8,128)(2,1)S(1)}, u32[]{:S(2)}) copy-start(bf16[1,8,128,128]{3,2,1,0:T(8,128)(2,1)S(1)} %collective-permute-done.2) | copy-start | bytes 786436
  3.1 2.4 %copy-start.14 = (s32[32,128]{1,0:T(8,128)S(1)}, s32[32,128]{1,0:T(8,128)}, u32[]{:S(2)}) copy-start(s32[32,128]{1,0:T(8,128)} %get-tuple-element.54) | copy-start | bytes 49156
  3.1 2.9 %copy-start.2 = (bf16[1,32,128,128]{3,2,1,0:T(8,128)(2,1)S(1)}, bf16[1,32,128,128]{3,2,1,0:T(8,128)(2,1)}, u32[]{:S(2)}) copy-start(bf16[1,32,128,128]{3,2,1,0:T(8,128)(2,1)} %param.8) | copy-start | bytes 3145732
  4.7 6.8 %copy-start.13 = (s32[3,1536]{1,0:T(4,128)S(1)}, s32[3,1536]{1,0:T(4,128)}, u32[]{:S(2)}) copy-start(s32[3,1536]{1,0:T(4,128)} %param.12) | copy-start | bytes 55300
  4.7 10.0 %collective-permute-start.6 = (bf16[3,16,128,128]{3,2,1,0:T(8,128)(2,1)S(1)}, bf16[3,16,128,128]{3,2,1,0:T(8,128)(2,1)}, u32[]{:S(2)}, u32[]{:S(2)}) collective-permute-start(bf16[3,16,128,128]{3,2,1,0:T(8,128)(2,1)S(1)} %constant_dynamic-slice_fusion.4), channel_id=1, source_target_pairs={{0,4},{4,0},{8,12},{12,8},{16,20},{20,16},{24,28},{28,24},{1,5},{5... | collective-permute-start | bytes 4718600 | tf_op jit(solution)/shard_map/ppermute | solution.py:201
  6.1 11.1 %collective-permute-start.4 = (bf16[8,128,128]{2,1,0:T(8,128)(2,1)S(1)}, bf16[8,128,128]{2,1,0:T(8,128)(2,1)S(1)}, u32[]{:S(2)}, u32[]{:S(2)}) collective-permute-start(bf16[8,128,128]{2,1,0:T(8,128)(2,1)S(1)} %get-tuple-element.48), channel_id=1, source_target_pairs={{0,8},{4,12},{8,0},{12,4},{16,24},{20,28},{24,16},{28,20},{1,9},{5... | collective-permute-start | bytes 786440 | tf_op jit(solution)/shard_map/ppermute | solution.py:201
  8.8 9.2 %collective-permute-start.5 = (bf16[8,128,128]{2,1,0:T(8,128)(2,1)S(1)}, bf16[8,128,128]{2,1,0:T(8,128)(2,1)S(1)}, u32[]{:S(2)}, u32[]{:S(2)}) collective-permute-start(bf16[8,128,128]{2,1,0:T(8,128)(2,1)S(1)} %get-tuple-element.49), channel_id=1, source_target_pairs={{0,16},{4,20},{8,24},{12,28},{16,0},{20,4},{24,8},{28,12},{1,17},{... | collective-permute-start | bytes 786440 | tf_op jit(solution)/shard_map/ppermute | solution.py:201
  10.9 10.7 %collective-permute-start.8 = (bf16[8,128,128]{2,1,0:T(8,128)(2,1)S(1)}, bf16[8,128,128]{2,1,0:T(8,128)(2,1)S(1)}, u32[]{:S(2)}, u32[]{:S(2)}) collective-permute-start(bf16[8,128,128]{2,1,0:T(8,128)(2,1)S(1)} %get-tuple-element.57), channel_id=1, source_target_pairs={{0,8},{4,12},{8,0},{12,4},{16,24},{20,28},{24,16},{28,20},{1,9},{5... | collective-permute-start | bytes 786440 | tf_op jit(solution)/shard_map/ppermute | solution.py:201
  11.5 12.1 %collective-permute-start.7 = (bf16[8,128,128]{2,1,0:T(8,128)(2,1)S(1)}, bf16[8,128,128]{2,1,0:T(8,128)(2,1)S(1)}, u32[]{:S(2)}, u32[]{:S(2)}) collective-permute-start(bf16[8,128,128]{2,1,0:T(8,128)(2,1)S(1)} %get-tuple-element.56), channel_id=1, source_target_pairs={{0,16},{4,20},{8,24},{12,28},{16,0},{20,4},{24,8},{28,12},{1,17},{... | collective-permute-start | bytes 786440 | tf_op jit(solution)/shard_map/ppermute | solution.py:201
  14.8 9.9 %copy-start = (f32[1536,128]{1,0:T(8,128)}, f32[1536,128]{1,0:T(8,128)S(1)}, u32[]{:S(2)}) copy-start(f32[1536,128]{1,0:T(8,128)S(1)} %add_multiply_fusion.tx_ref) | copy-start | bytes 2359300
  17.2 6.4 %copy-start.3 = (bf16[1,32,128,128]{3,2,1,0:T(8,128)(2,1)S(1)}, bf16[1,32,128,128]{3,2,1,0:T(8,128)(2,1)}, u32[]{:S(2)}) copy-start(bf16[1,32,128,128]{3,2,1,0:T(8,128)(2,1)} %param.8) | copy-start | bytes 3145732
  17.2 6.4 %copy-start.5 = (bf16[1,8,128,128]{3,2,1,0:T(8,128)(2,1)S(1)}, bf16[1,8,128,128]{3,2,1,0:T(8,128)(2,1)}, u32[]{:S(2)}) copy-start(bf16[1,8,128,128]{3,2,1,0:T(8,128)(2,1)} %copy-done.4) | copy-start | bytes 786436
  17.2 7.4 %copy-start.8 = (bf16[8,128,128]{2,1,0:T(8,128)(2,1)}, bf16[8,128,128]{2,1,0:T(8,128)(2,1)S(1)}, u32[]{:S(2)}) copy-start(bf16[8,128,128]{2,1,0:T(8,128)(2,1)S(1)} %collective-permute-done.4) | copy-start | bytes 786436
  18.0 6.6 %copy-start.6 = (bf16[8,128,128]{2,1,0:T(8,128)(2,1)}, bf16[8,128,128]{2,1,0:T(8,128)(2,1)S(1)}, u32[]{:S(2)}) copy-start(bf16[8,128,128]{2,1,0:T(8,128)(2,1)S(1)} %collective-permute-done.5) | copy-start | bytes 786436
  18.9 13.6 %collective-permute-start.9 = (bf16[8,128,128]{2,1,0:T(8,128)(2,1)}, bf16[8,128,128]{2,1,0:T(8,128)(2,1)}, u32[]{:S(2)}, u32[]{:S(2)}) collective-permute-start(bf16[8,128,128]{2,1,0:T(8,128)(2,1)} %get-tuple-element.62), channel_id=1, source_target_pairs={{0,8},{4,12},{8,0},{12,4},{16,24},{20,28},{24,16},{28,20},{1,9},{5... | collective-permute-start | bytes 786440 | tf_op jit(solution)/shard_map/ppermute | solution.py:201
  20.0 12.4 %collective-permute-start.10 = (bf16[8,128,128]{2,1,0:T(8,128)(2,1)}, bf16[8,128,128]{2,1,0:T(8,128)(2,1)}, u32[]{:S(2)}, u32[]{:S(2)}) collective-permute-start(bf16[8,128,128]{2,1,0:T(8,128)(2,1)} %get-tuple-element.63), channel_id=1, source_target_pairs={{0,16},{4,20},{8,24},{12,28},{16,0},{20,4},{24,8},{28,12},{1,17},{... | collective-permute-start | bytes 786440 | tf_op jit(solution)/shard_map/ppermute | solution.py:201
  21.6 3.0 %copy-start.9 = (bf16[8,128,128]{2,1,0:T(8,128)(2,1)}, bf16[8,128,128]{2,1,0:T(8,128)(2,1)S(1)}, u32[]{:S(2)}) copy-start(bf16[8,128,128]{2,1,0:T(8,128)(2,1)S(1)} %collective-permute-done.8) | copy-start | bytes 786436
  23.6 1.0 %copy-start.11 = (bf16[8,128,128]{2,1,0:T(8,128)(2,1)}, bf16[8,128,128]{2,1,0:T(8,128)(2,1)S(1)}, u32[]{:S(2)}) copy-start(bf16[8,128,128]{2,1,0:T(8,128)(2,1)S(1)} %collective-permute-done.7) | copy-start | bytes 786436
  32.4 1.6 %copy-start.7 = (bf16[8,128,128]{2,1,0:T(8,128)(2,1)S(1)}, bf16[8,128,128]{2,1,0:T(8,128)(2,1)}, u32[]{:S(2)}) copy-start(bf16[8,128,128]{2,1,0:T(8,128)(2,1)} %copy-done.6) | copy-start | bytes 786436
  32.4 1.6 %copy-start.10 = (bf16[8,128,128]{2,1,0:T(8,128)(2,1)S(1)}, bf16[8,128,128]{2,1,0:T(8,128)(2,1)}, u32[]{:S(2)}) copy-start(bf16[8,128,128]{2,1,0:T(8,128)(2,1)} %copy-done.9) | copy-start | bytes 786436
  32.4 1.6 %copy-start.12 = (bf16[8,128,128]{2,1,0:T(8,128)(2,1)S(1)}, bf16[8,128,128]{2,1,0:T(8,128)(2,1)}, u32[]{:S(2)}) copy-start(bf16[8,128,128]{2,1,0:T(8,128)(2,1)} %get-tuple-element.68) | copy-start | bytes 786436
  34.0 1.3 %copy-start.1 = (f32[1536,128]{1,0:T(8,128)S(1)}, f32[1536,128]{1,0:T(8,128)}, u32[]{:S(2)}) copy-start(f32[1536,128]{1,0:T(8,128)} %copy-done) | copy-start | bytes 2359300
  40.9 11.9 %copy-start.15 = (f32[16,128]{1,0:T(8,128)S(1)}, f32[16,128]{1,0:T(8,128)}, u32[]{:S(2)}) copy-start(f32[16,128]{1,0:T(8,128)} %get-tuple-element.70) | copy-start | bytes 24580
  46.7 1.4 %collective-permute-start.11 = (f32[9,1536]{1,0:T(8,128)S(1)}, f32[9,1536]{1,0:T(8,128)S(1)}, u32[]{:S(2)}, u32[]{:S(2)}) collective-permute-start(f32[9,1536]{1,0:T(8,128)S(1)} %fusion.24), channel_id=1, source_target_pairs={{0,4},{4,0},{8,12},{12,8},{16,20},{20,16},{24,28},{28,24},{1,5},{5... | collective-permute-start | bytes 165896 | tf_op jit(solution)/shard_map/ppermute | solution.py:201
  48.1 5.7 %collective-permute-start.14 = (bf16[9,1536]{1,0:T(8,128)(2,1)S(1)}, bf16[9,1536]{1,0:T(8,128)(2,1)S(1)}, u32[]{:S(2)}, u32[]{:S(2)}) collective-permute-start(bf16[9,1536]{1,0:T(8,128)(2,1)S(1)} %fusion.39), channel_id=1, source_target_pairs={{0,3},{1,0},{2,1},{3,2},{4,7},{5,4},{6,5},{7,6},{8,11},{9,8},{10,9... | collective-permute-start | bytes 82952 | tf_op jit(solution)/shard_map/ppermute | solution.py:335
  51.7 5.3 %collective-permute-start.13 = (bf16[9,1536]{1,0:T(8,128)(2,1)S(1)}, bf16[9,1536]{1,0:T(8,128)(2,1)S(1)}, u32[]{:S(2)}, u32[]{:S(2)}) collective-permute-start(bf16[9,1536]{1,0:T(8,128)(2,1)S(1)} %fusion.39), channel_id=1, source_target_pairs={{0,2},{1,3},{2,0},{3,1},{4,6},{5,7},{6,4},{7,5},{8,10},{9,11},{10,... | collective-permute-start | bytes 82952 | tf_op jit(solution)/shard_map/ppermute | solution.py:335
  51.8 5.9 %collective-permute-start.12 = (bf16[9,1536]{1,0:T(8,128)(2,1)S(1)}, bf16[9,1536]{1,0:T(8,128)(2,1)S(1)}, u32[]{:S(2)}, u32[]{:S(2)}) collective-permute-start(bf16[9,1536]{1,0:T(8,128)(2,1)S(1)} %fusion.39), channel_id=1, source_target_pairs={{0,1},{1,2},{2,3},{3,0},{4,5},{5,6},{6,7},{7,4},{8,9},{9,10},{10,1... | collective-permute-start | bytes 82952 | tf_op jit(solution)/shard_map/ppermute | solution.py:335
  57.8 4.8 %collective-permute-start.17 = (bf16[9,768]{1,0:T(8,128)(2,1)S(1)}, bf16[9,768]{1,0:T(8,128)(2,1)S(1)}, u32[]{:S(2)}, u32[]{:S(2)}) collective-permute-start(bf16[9,768]{1,0:T(8,128)(2,1)S(1)} %get-tuple-element.130), channel_id=1, source_target_pairs={{0,24},{4,28},{8,16},{12,20},{16,8},{20,12},{24,0},{28,4},{1,25},{... | collective-permute-start | bytes 41480 | tf_op jit(solution)/shard_map/ppermute | solution.py:201
  59.3 3.8 %collective-permute-start.16 = (bf16[9,768]{1,0:T(8,128)(2,1)S(1)}, bf16[9,768]{1,0:T(8,128)(2,1)S(1)}, u32[]{:S(2)}, u32[]{:S(2)}) collective-permute-start(bf16[9,768]{1,0:T(8,128)(2,1)S(1)} %get-tuple-element.129), channel_id=1, source_target_pairs={{0,16},{4,20},{8,24},{12,28},{16,0},{20,4},{24,8},{28,12},{1,17},{... | collective-permute-start | bytes 41480 | tf_op jit(solution)/shard_map/ppermute | solution.py:201
  59.9 3.8 %collective-permute-start.15 = (bf16[9,768]{1,0:T(8,128)(2,1)S(1)}, bf16[9,768]{1,0:T(8,128)(2,1)S(1)}, u32[]{:S(2)}, u32[]{:S(2)}) collective-permute-start(bf16[9,768]{1,0:T(8,128)(2,1)S(1)} %get-tuple-element.128), channel_id=1, source_target_pairs={{0,8},{4,12},{8,0},{12,4},{16,24},{20,28},{24,16},{28,20},{1,9},{5... | collective-permute-start | bytes 41480 | tf_op jit(solution)/shard_map/ppermute | solution.py:201
  63.9 1.3 %collective-permute-start.18 = (bf16[36,576]{1,0:T(8,128)(2,1)S(1)}, bf16[36,576]{1,0:T(8,128)(2,1)S(1)}, u32[]{:S(2)}, u32[]{:S(2)}) collective-permute-start(bf16[36,576]{1,0:T(8,128)(2,1)S(1)} %pad_maximum_fusion.3), channel_id=1, source_target_pairs={{0,4},{4,0},{8,12},{12,8},{16,20},{20,16},{24,28},{28,24},{1,5},{5... | collective-permute-start | bytes 124424 | tf_op jit(solution)/shard_map/ppermute | solution.py:201
